TPU v7x, 1024 devices: a whole 4x4x32 slice. The times are simulated.
1024 devices in a mesh: dp: 64 (over z, core), mp: 16 (over x, y).
Axes of the slice: x: 4, y: 4, z: 32, core: 2. Of those that a mesh axis runs over, the one named last changes fastest.
Arguments:
- queries: bfloat16 [32768, 4096], P('dp', 'mp'), may hold values from -6 to 6
- keys: bfloat16 [32768, 512], P('dp'), may hold values from -6 to 6
- values: bfloat16 [32768, 512], P('dp'), may hold values from -6 to 6
- attn_out: bfloat16 [32768, 4096], P('dp', 'mp'), may hold values from -4 to 4
- out_grad: bfloat16 [32768, 4096], P('dp', 'mp'), may hold values from -4 to 4
- lse: bfloat16 [32768, 32], P('dp', 'mp'), may hold values from 0 to 3
- layer_grad: bfloat16 [32768, 4096], P('dp'), may hold values from -0.3125 to 0.3125
- feedback: bfloat16 [64, 4096, 4096], P('dp', None, 'mp'), may hold values from -0.29882812 to 0.29882812
- doc_lengths: int32 [64, 8], P('dp'), may hold values from 1 to 256, 512 in all within a row
- src_order: int32 [64, 64], P('dp'), may hold values from 0 to 63, each once within a row
- dst_order: int32 [64, 64], P('dp'), may hold values from 0 to 63, each once within a row
Outputs:
- query_grad: bfloat16 [32768, 4096], P('dp', 'mp')
- kv_grad: bfloat16 [32768, 1024], P(('dp', 'mp'))
- weight_grad: float32 [4096, 4096], P('dp', 'mp')
Inputs may be any that keep to these rules, and one draw needn't show every extreme that they name: Each row of src_order is a permutation: replica r sends exactly one block to each replica d, its block src_order[r, d]. Each row of dst_order is a permutation: every replica receives exactly one block from each replica. `doc_lengths`: each row sums to 512.
All inputs are finite; a program needn't handle non-finite values.
Results may differ from a plain program's by a relative error of at most 0.0095.
Values may be sent and summed in bfloat16 or wider, within the bound.
A program may use at most 64 MiB of HBM per device.

v0:
```python
import jax
import jax.numpy as jnp
from jax import lax
from jax.sharding import PartitionSpec as P

HPD = 2
GROUP = 8
CR = 8


def quantize_spans(term):
    count_rows, columns = term.shape
    spans = term.reshape(count_rows // CR, CR, columns)
    top = jnp.max(jnp.abs(spans), axis=(1, 2), keepdims=True) + 1e-06
    scales = top.astype(jnp.bfloat16)
    levels = (spans / scales.astype(jnp.float32)).astype(jnp.bfloat16)
    return (levels, scales)


def body(
    queries,
    keys,
    values,
    attn_out,
    out_grad,
    lse,
    layer_grad,
    feedback,
    doc_lengths,
    src_order,
    dst_order,
):
    replicas = lax.axis_size("dp")
    row_count = queries.shape[0]
    head_cols = queries.shape[1]
    kv_width = keys.shape[1]
    out_width = layer_grad.shape[1]
    block_rows = row_count // replicas
    head_dim = head_cols // HPD
    factor = head_dim ** (-0.5)
    model_index = lax.axis_index("mp")
    group_index = model_index * HPD // GROUP
    carried = feedback[0]
    owned_rows = out_width // replicas
    carried_rows = carried.astype(jnp.float32)
    term = (
        jnp.einsum("td,tc->dc", layer_grad, attn_out, preferred_element_type=jnp.float32)
        + carried_rows
    )
    levels, scales = quantize_spans(term)
    levels = lax.optimization_barrier(levels)
    weight_grad = lax.psum_scatter(
        (levels.astype(jnp.float32) * scales.astype(jnp.float32)).reshape(
            owned_rows * lax.axis_size("dp"), head_cols
        ),
        "dp",
        scatter_dimension=0,
        tiled=True,
    )
    kv_pair = jnp.concatenate(
        [
            lax.dynamic_slice_in_dim(keys, group_index * head_dim, head_dim, 1),
            lax.dynamic_slice_in_dim(values, group_index * head_dim, head_dim, 1),
        ],
        axis=1,
    )
    send_order = src_order[0]
    take_order = dst_order[0]

    def to_blocks(array):
        return jnp.take(array.reshape(replicas, block_rows, array.shape[1]), send_order, axis=0)

    def from_blocks(array):
        return jnp.take(array, take_order, axis=0).reshape(row_count, array.shape[2])

    loader_delta = jnp.sum(
        out_grad.reshape(row_count, HPD, head_dim).astype(jnp.float32)
        * attn_out.reshape(row_count, HPD, head_dim).astype(jnp.float32),
        axis=-1,
    )
    arrived = (
        lax.all_to_all(to_blocks(queries), "dp", split_axis=0, concat_axis=0, tiled=True),
        lax.all_to_all(to_blocks(kv_pair), "dp", split_axis=0, concat_axis=0, tiled=True),
        lax.all_to_all(to_blocks(out_grad), "dp", split_axis=0, concat_axis=0, tiled=True),
    )
    stats = (
        lax.all_to_all(
            to_blocks(lse.astype(jnp.float32)), "dp", split_axis=0, concat_axis=0, tiled=True
        ),
        lax.all_to_all(to_blocks(loader_delta), "dp", split_axis=0, concat_axis=0, tiled=True),
    )
    q_moved = from_blocks(arrived[0])
    kv_moved = from_blocks(arrived[1])
    do_moved = from_blocks(arrived[2])
    lse_moved = from_blocks(stats[0])
    delta = from_blocks(stats[1])
    key_head = kv_moved[:, :head_dim]
    value_head = kv_moved[:, head_dim:]
    lengths = doc_lengths[0]
    ends = jnp.cumsum(lengths)
    positions = jnp.arange(row_count, dtype=jnp.int32)
    segment = jnp.sum((positions[:, None] >= ends[None, :]).astype(jnp.int32), axis=1)
    allowed = (segment[:, None] == segment[None, :]) & (positions[None, :] <= positions[:, None])
    q_heads = q_moved.reshape(row_count, HPD, head_dim)
    do_heads = do_moved.reshape(row_count, HPD, head_dim)
    scores = (
        jnp.einsum("qhd,kd->hqk", q_heads, key_head, preferred_element_type=jnp.float32) * factor
    )
    probs = jnp.where(allowed[None], jnp.exp(scores - lse_moved.T[:, :, None]), 0.0)
    probs_low = probs.astype(jnp.bfloat16)
    value_part = jnp.einsum("hqk,qhd->kd", probs_low, do_heads, preferred_element_type=jnp.float32)
    dprobs = jnp.einsum("qhd,kd->hqk", do_heads, value_head, preferred_element_type=jnp.float32)
    dscores_low = (probs * (dprobs - delta.T[:, :, None]) * factor).astype(jnp.bfloat16)
    query_grad = jnp.einsum(
        "hqk,kd->qhd", dscores_low, key_head, preferred_element_type=jnp.float32
    )
    query_grad = query_grad.astype(jnp.bfloat16).reshape(row_count, head_cols)
    key_part = jnp.einsum("hqk,qhd->kd", dscores_low, q_heads, preferred_element_type=jnp.float32)
    partial_terms = jnp.zeros((row_count, 2 * kv_width), jnp.float32)
    partial_terms = lax.dynamic_update_slice(partial_terms, key_part, (0, group_index * head_dim))
    partial_terms = lax.dynamic_update_slice(
        partial_terms, value_part, (0, kv_width + group_index * head_dim)
    )
    kv_grad = lax.psum_scatter(partial_terms, "mp", scatter_dimension=0, tiled=True).astype(
        jnp.bfloat16
    )
    return (query_grad, kv_grad, weight_grad)


def solution(mesh):
    return jax.shard_map(
        body,
        mesh=mesh,
        in_specs=(
            P("dp", "mp"),
            P("dp", None),
            P("dp", None),
            P("dp", "mp"),
            P("dp", "mp"),
            P("dp", "mp"),
            P("dp", None),
            P("dp", None, "mp"),
            P("dp", None),
            P("dp", None),
            P("dp", None),
        ),
        out_specs=(P("dp", "mp"), P(("dp", "mp"), None), P("dp", "mp")),
        check_vma=False,
    )
```

profile of v0, /device:TPU:1, one launch (start us, length us, event | category | flops | bytes accessed | tf_op | source)
XLA Modules:
  0.0 561.9 jit_solution(5561279158170599623)
XLA Ops:
  7.2 0.7 compare_and_fusion.1
  8.6 0.8 reshape.149
  9.4 1.1 convert_multiply_fusion
  13.2 0.8 broadcast_select_fusion.7
  13.9 30.4 %all-to-all-start.4 = ((f32[64,8,2]{1,2,0:T(2,128)}), f32[64,8,2]{1,2,0:T(2,128)S(1)}, u32[]{:S(2)}, u32[]{:S(2)}) async-start(f32[64,8,2]{1,2,0:T(2,128)} %get-tuple-element.31), calls=%async_computation.4 | async-start | bytes 131072 | tf_op jit(solution)/shard_map/all_to_all | solution.py:90
  44.4 1.0 constant_dynamic-slice_fusion
  47.3 22.0 %all-to-all-done.4 = f32[64,8,2]{1,2,0:T(2,128)S(1)} async-done(((f32[64,8,2]{1,2,0:T(2,128)}), f32[64,8,2]{1,2,0:T(2,128)S(1)}, u32[]{:S(2)}, u32[]{:S(2)}) %all-to-all-start.4) | async-done | bytes 4128 | tf_op jit(solution)/shard_map/all_to_all | solution.py:90
  69.3 5.9 %all-to-all-start.2 = ((f32[64,8,2]{1,2,0:T(2,128)}), f32[64,8,2]{1,2,0:T(2,128)S(1)}, u32[]{:S(2)}, u32[]{:S(2)}) async-start(f32[64,8,2]{1,2,0:T(2,128)} %get-tuple-element.32), calls=%async_computation.2 | async-start | bytes 131072 | tf_op jit(solution)/shard_map/all_to_all | solution.py:87
  75.2 0.9 broadcast_select_fusion.2
  76.1 24.3 %all-to-all-done.2 = f32[64,8,2]{1,2,0:T(2,128)S(1)} async-done(((f32[64,8,2]{1,2,0:T(2,128)}), f32[64,8,2]{1,2,0:T(2,128)S(1)}, u32[]{:S(2)}, u32[]{:S(2)}) %all-to-all-start.2) | async-done | bytes 4128 | tf_op jit(solution)/shard_map/all_to_all | solution.py:87
  100.4 46.4 %all_to_all.25 = bf16[64,8,256]{2,1,0:T(8,128)(2,1)S(1)} all-to-all(bf16[64,8,256]{2,1,0:T(8,128)(2,1)S(1)} %get-tuple-element.26), channel_id=1, replica_groups=mesh['dp'=64,'mp'=16] {'dp'}, dimensions={0} | all-to-all | bytes 524288 | tf_op jit(solution)/shard_map/all_to_all | solution.py:84
  146.8 47.1 %all_to_all.26 = bf16[64,8,256]{2,1,0:T(8,128)(2,1)S(1)} all-to-all(bf16[64,8,256]{2,1,0:T(8,128)(2,1)S(1)} %get-tuple-element.27), channel_id=1, replica_groups=mesh['dp'=64,'mp'=16] {'dp'}, dimensions={0} | all-to-all | bytes 524288 | tf_op jit(solution)/shard_map/all_to_all | solution.py:82
  193.8 6.5 %all-to-all-start = ((bf16[64,8,256]{2,1,0:T(8,128)(2,1)}), bf16[64,8,256]{2,1,0:T(8,128)(2,1)S(1)}, u32[]{:S(2)}, u32[]{:S(2)}) async-start(bf16[64,8,256]{2,1,0:T(8,128)(2,1)} %get-tuple-element.28), calls=%async_computation | async-start | bytes 524288 | tf_op jit(solution)/shard_map/all_to_all | solution.py:83
  203.8 38.0 %all-to-all-done = bf16[64,8,256]{2,1,0:T(8,128)(2,1)S(1)} async-done(((bf16[64,8,256]{2,1,0:T(8,128)(2,1)}), bf16[64,8,256]{2,1,0:T(8,128)(2,1)S(1)}, u32[]{:S(2)}, u32[]{:S(2)}) %all-to-all-start) | async-done | bytes 262176 | tf_op jit(solution)/shard_map/all_to_all | solution.py:83
  242.7 0.7 fusion.5
  245.3 1.3 copy-done.1
  246.9 6.5 %abs_reduce_fusion = (f32[4096]{0:T(1024)S(1)}, f32[4096,256]{1,0:T(8,128)}) fusion(bf16[1,4096,256]{2,1,0:T(8,128)(2,1)} %param.22, bf16[512,4096]{1,0:T(8,128)(2,1)} %param.21, bf16[512,256]{1,0:T(8,128)(2,1)} %param.18), kind=kOutput, calls=%fused_computation.14 | convolution fusion | flops 1077932032 | bytes 10764288 | tf_op jit(solution)/shard_map/td,tc->dc/dot_general | solution.py:47
  253.7 3.1 fusion
  256.9 2.8 multiply_bitcast_fusion
  259.7 0.9 copy-done.8
  261.0 0.8 copy.71
  261.8 76.3 %reduce-scatter.3.cloned.1.call-done = f32[32,1024]{1,0:T(8,128)} async-done(((f32[512,1024]{1,0:T(8,128)}), f32[32,1024]{1,0:T(8,128)}) %reduce-scatter.3.cloned.1.call-update) | async-done | bytes 131088 | tf_op jit(solution)/shard_map/reduce_scatter | solution.py:124
  338.1 1.5 convert_element_type.63
  339.6 215.5 %reduce-scatter.5.cloned.1.call-done = f32[64,256]{1,0:T(8,128)} async-done(((f32[4096,256]{1,0:T(8,128)}), f32[64,256]{1,0:T(8,128)}) %reduce-scatter.5.cloned.1.call-update) | async-done | bytes 65552 | tf_op jit(solution)/shard_map/reduce_scatter | solution.py:52
  (63 shorter events, 12.2 us)
Async XLA Ops:
  7.2 39.5 %copy-start = (bf16[512,256]{1,0:T(8,128)(2,1)S(1)}, bf16[512,256]{1,0:T(8,128)(2,1)}, u32[]{:S(2)}) copy-start(bf16[512,256]{1,0:T(8,128)(2,1)} %param.15) | copy-start | bytes 786436
  10.8 35.3 %copy-start.4 = (bf16[512,256]{1,0:T(8,128)(2,1)S(1)}, bf16[512,256]{1,0:T(8,128)(2,1)}, u32[]{:S(2)}) copy-start(bf16[512,256]{1,0:T(8,128)(2,1)} %param.19) | copy-start | bytes 786436
  13.9 55.4 %all-to-all-start.4 = ((f32[64,8,2]{1,2,0:T(2,128)}), f32[64,8,2]{1,2,0:T(2,128)S(1)}, u32[]{:S(2)}, u32[]{:S(2)}) async-start(f32[64,8,2]{1,2,0:T(2,128)} %get-tuple-element.31), calls=%async_computation.4 | async-start | bytes 131072 | tf_op jit(solution)/shard_map/all_to_all | solution.py:90
  46.0 154.4 %copy-start.9 = (s32[1,8]{1,0:T(1,128)S(1)}, s32[1,8]{1,0:T(1,128)}, u32[]{:S(2)}) copy-start(s32[1,8]{1,0:T(1,128)} %param.23) | copy-start | bytes 100
  46.0 154.6 %copy-start.10 = (s32[1,64]{1,0:T(1,128)S(1)}, s32[1,64]{1,0:T(1,128)}, u32[]{:S(2)}) copy-start(s32[1,64]{1,0:T(1,128)} %param.25) | copy-start | bytes 772
  69.3 31.1 %all-to-all-start.2 = ((f32[64,8,2]{1,2,0:T(2,128)}), f32[64,8,2]{1,2,0:T(2,128)S(1)}, u32[]{:S(2)}, u32[]{:S(2)}) async-start(f32[64,8,2]{1,2,0:T(2,128)} %get-tuple-element.32), calls=%async_computation.2 | async-start | bytes 131072 | tf_op jit(solution)/shard_map/all_to_all | solution.py:87
  193.8 47.9 %all-to-all-start = ((bf16[64,8,256]{2,1,0:T(8,128)(2,1)}), bf16[64,8,256]{2,1,0:T(8,128)(2,1)S(1)}, u32[]{:S(2)}, u32[]{:S(2)}) async-start(bf16[64,8,256]{2,1,0:T(8,128)(2,1)} %get-tuple-element.28), calls=%async_computation | async-start | bytes 524288 | tf_op jit(solution)/shard_map/all_to_all | solution.py:83
  200.3 137.7 %reduce-scatter.3.cloned.1.call-start = ((), (), s32[]{:S(2)}) async-start(), calls=%async_computation.7 | async-start | bytes 2228224 | tf_op jit(solution)/shard_map/reduce_scatter | solution.py:124
  242.5 0.9 copy-start.7
  242.6 0.8 copy-start.2
  242.7 0.7 copy-start.5
  243.4 1.0 copy-start.6
  243.9 1.0 copy-start.3
  245.3 1.3 copy-start.1
  246.6 308.4 %reduce-scatter.5.cloned.1.call-start = ((), (), s32[]{:S(2)}) async-start(), calls=%async_computation.8 | async-start | bytes 4259840 | tf_op jit(solution)/shard_map/reduce_scatter | solution.py:52
  259.7 0.9 copy-start.8
Sparse Core Ops, SparseCore 0:
  246.8 91.2 reduce-scatter.2
  342.4 212.6 reduce-scatter.4
where the time goes:
time: 565 us; the launch traced here: 562 us
  waiting for transfers between devices  376 us (67%)
  blocking collectives  93.5 us (17%)
  starting transfers between devices  43 us (8%)
  between operations  14.4 us (3%)
  other arithmetic  13.1 us (2%)
  local copies, waits for them, and re-layouts  12.9 us (2%)
  matrix products  8.86 us (2%)
    reduce_scatter x1, waiting for transfers between devices, body(): lax.psum_scatter((levels.astype(jnp.float32) * scales.astype(jnp.float32)...  215 us
    reduce_scatter x1, waiting for transfers between devices, body(): lax.psum_scatter(partial_terms, 'mp', scatter_dimension=0, tiled=True)  76.3 us
    all_to_all x1, blocking collectives, body(): lax.all_to_all(to_blocks(queries), 'dp', split_axis=0, concat_axis=0, til...  47.1 us
    all_to_all x1, blocking collectives, body(): lax.all_to_all(to_blocks(out_grad), 'dp', split_axis=0, concat_axis=0, ti...  46.4 us
    all_to_all x1, waiting for transfers between devices, body(): lax.all_to_all(to_blocks(kv_pair), 'dp', split_axis=0, concat_axis=0, til...  38 us
    all_to_all x1, starting transfers between devices, body(): lax.all_to_all(to_blocks(loader_delta), 'dp', split_axis=0, concat_axis=0...  30.4 us
    all_to_all x1, waiting for transfers between devices, body(): lax.all_to_all(to_blocks(lse.astype(jnp.float32)), 'dp', split_axis=0, co...  24.3 us
    all_to_all x1, waiting for transfers between devices, body(): lax.all_to_all(to_blocks(loader_delta), 'dp', split_axis=0, concat_axis=0...  22 us
  transfers between devices with their start and end apart: 5, of which 5 were waited for; matrix products, arithmetic and copies ran while one was open for 4% of the time, Pallas kernels for 0%

commit v1 on v0

v1 whole, which is shorter than its diff:
```python
import functools

import jax
import jax.numpy as jnp
from jax import lax
from jax.experimental import pallas as pl
from jax.experimental.pallas import tpu as pltpu
from jax.sharding import PartitionSpec as P

HD = 128
HPD = 2
GROUP = 8
CR = 8
BR = 8
SHARE = GROUP // HPD
STRIDE = 29
FIRST = 16
MESH = pl.DeviceIdType.MESH


def whole_wait(ref, sem):
    pltpu.make_async_copy(ref, ref, sem).wait()


def kernel(
    n,
    nm,
    src_ref,
    dst_ref,
    len_ref,
    q_ref,
    do_ref,
    o3_ref,
    o_ref,
    lse_ref,
    k_hbm,
    v_hbm,
    lg_hbm,
    fb_hbm,
    qg_ref,
    kvg_ref,
    wg_ref,
    kv_in,
    lg_v,
    fb_v,
    st_cols,
    st_rows,
    qd_send,
    qd_recv,
    kv_send,
    kv_recv,
    st_send,
    st_recv,
    own,
    p_send,
    p_recv,
    r_send,
    r_recv,
    l_send,
    l_recv,
    m_q,
    m_do,
    m_kv,
    dkv,
    g_send,
    g_recv,
    loc_sem,
    qd_s,
    qd_r,
    kv_s,
    kv_r,
    st_s,
    st_r,
    yf_s,
    yf_r,
    p_s,
    p_r,
    r_s,
    r_r,
    l_s,
    l_r,
    g_s,
    g_r,
):
    f32, bf16 = jnp.float32, jnp.bfloat16
    me = lax.axis_index("dp")
    mp = lax.axis_index("mp")
    group, y = mp // SHARE, mp % SHARE
    z, core = me // 2, me % 2
    nz = n // 2
    rows = n * BR
    right_hops, left_hops = nz // 2, nz // 2 - 1
    per_class = n // SHARE

    column = pl.ds(pl.multiple_of(group * HD, HD), HD)
    k_copy = pltpu.make_async_copy(k_hbm.at[:, :, column], kv_in.at[0], loc_sem.at[0])
    v_copy = pltpu.make_async_copy(v_hbm.at[:, :, column], kv_in.at[1], loc_sem.at[1])
    lg_copy = pltpu.make_async_copy(lg_hbm, lg_v, loc_sem.at[2])
    fb_copy = pltpu.make_async_copy(fb_hbm, fb_v, loc_sem.at[3])
    k_copy.start()
    v_copy.start()
    lg_copy.start()
    fb_copy.start()

    barrier = pltpu.get_barrier_semaphore()

    def greet_dp(k, _):
        pl.semaphore_signal(barrier, 1, device_id=((me + k) % n, mp), device_id_type=MESH)
        return 0

    def greet_mp(k, _):
        pl.semaphore_signal(barrier, 1, device_id=(me, (mp + k) % nm), device_id_type=MESH)
        return 0

    lax.fori_loop(1, n, greet_dp, 0)
    lax.fori_loop(1, nm, greet_mp, 0)

    product = (do_ref[...].astype(f32) * o3_ref[...].astype(f32)).reshape(rows, HPD * HD)
    delta0 = jnp.sum(product[:, :HD], axis=1, keepdims=True)
    delta1 = jnp.sum(product[:, HD:], axis=1, keepdims=True)
    lse = lse_ref[...]
    lane = lax.broadcasted_iota(jnp.int32, (rows, HD), 1)
    st_cols[...] = jnp.where(
        lane == 0,
        lse[:, 0:1],
        jnp.where(
            lane == 1,
            lse[:, 1:2],
            jnp.where(lane == 2, delta0, jnp.where(lane == 3, delta1, 0.0)),
        ),
    )
    packed = st_cols[pl.ds(0, n, stride=BR), :]
    for r in range(1, BR):
        packed = packed + pltpu.roll(st_cols[pl.ds(r, n, stride=BR), :], 4 * r, 1)
    st_rows[...] = packed

    k_copy.wait()
    v_copy.wait()

    def pack(d, _):
        block = src_ref[0, d]
        kv_send[d] = jnp.concatenate([kv_in[0, block], kv_in[1, block]], axis=0)
        st_send[d] = st_rows[pl.ds(block, 1), :]
        qb = q_ref[block]
        db = do_ref[block]
        qd_send[d] = jnp.concatenate([qb[:, :HD], qb[:, HD:], db[:, :HD], db[:, HD:]], axis=0)
        return 0

    lax.fori_loop(0, n, pack, 0)

    pl.semaphore_wait(barrier, n - 1 + nm - 1)

    def kv_slot(source, dest):
        return ((source + dest) % SHARE) * per_class + source // SHARE

    own_slot = kv_slot(me, me)
    has_self = (me + me) % SHARE == y

    def send_kv(j, _):
        d = SHARE * ((me // SHARE + j) % per_class) + (y + SHARE - me % SHARE) % SHARE
        slot = y * per_class + me // SHARE

        @pl.when(d == me)
        def _():
            pltpu.make_async_copy(kv_send.at[me], kv_recv.at[slot], kv_r).start()

        @pl.when(d != me)
        def _():
            pltpu.make_async_remote_copy(
                kv_send.at[d], kv_recv.at[slot], kv_s, kv_r, device_id=(d, mp), device_id_type=MESH
            ).start()

        return 0

    lax.fori_loop(0, per_class, send_kv, 0)

    pltpu.make_async_copy(qd_send.at[me], qd_recv.at[me], qd_r).start()
    pltpu.make_async_copy(st_send.at[me], st_recv.at[me], st_r).start()

    def send_block(t, _):
        d = (me + t * STRIDE) % n
        pltpu.make_async_remote_copy(
            qd_send.at[d], qd_recv.at[me], qd_s, qd_r, device_id=(d, mp), device_id_type=MESH
        ).start()
        pltpu.make_async_remote_copy(
            st_send.at[d], st_recv.at[me], st_s, st_r, device_id=(d, mp), device_id_type=MESH
        ).start()
        return 0

    first = min(FIRST, n)
    lax.fori_loop(1, first, send_block, 0)
    per_step = -(-(n - first) // right_hops)

    lg_copy.wait()
    fb_copy.wait()
    partner = me + 1 - 2 * core

    def partner_copy(g):
        return pltpu.make_async_remote_copy(
            p_send.at[pl.ds(2 * g, 2)],
            p_recv.at[pl.ds(2 * g, 2)],
            p_s.at[g],
            p_r.at[g],
            device_id=(partner, mp),
            device_id_type=MESH,
        )

    def make_term(g, _):
        start = pl.multiple_of(g * 256, 256)
        term = lax.dot_general(
            lg_v[:, pl.ds(start, 256)],
            o_ref[...],
            (((0,), (0,)), ((), ())),
            preferred_element_type=f32,
        )
        term = term + fb_v[pl.ds(start, 256), :].astype(f32)
        spans = term.reshape(256 // CR, CR, HPD * HD)
        top = jnp.max(jnp.max(jnp.abs(spans), axis=1, keepdims=True), axis=2, keepdims=True)
        scale = (top + 1e-06).astype(bf16).astype(f32)
        level = (spans / scale).astype(bf16).astype(f32)
        value = (level * scale).reshape(4, 64, HPD * HD)
        for chip in range(2):
            even, odd = value[2 * chip], value[2 * chip + 1]
            own[2 * g + chip] = jnp.where(core == 0, even, odd)
            p_send[2 * g + chip] = jnp.where(core == 0, odd, even).astype(bf16)
        partner_copy(g).start()
        return 0

    lax.fori_loop(0, nz // 2, make_term, 0)

    def partner_wait(g, _):
        partner_copy(g).wait()
        return 0

    lax.fori_loop(0, nz // 2, partner_wait, 0)

    def right_copy(s):
        return pltpu.make_async_remote_copy(
            r_send.at[s],
            r_recv.at[s],
            r_s.at[s],
            r_r.at[s],
            device_id=(((z + 1) % nz) * 2 + core, mp),
            device_id_type=MESH,
        )

    def left_copy(s):
        return pltpu.make_async_remote_copy(
            l_send.at[s],
            l_recv.at[s],
            l_s.at[s],
            l_r.at[s],
            device_id=(((z + nz - 1) % nz) * 2 + core, mp),
            device_id_type=MESH,
        )

    def own_sum(chip):
        return own[chip] + p_recv[chip].astype(f32)

    def more_blocks(s):
        begin = jnp.minimum(first + s * per_step, n)
        end = jnp.minimum(begin + per_step, n)
        lax.fori_loop(begin, end, send_block, 0)

    r_send[0] = own_sum((z + right_hops) % nz).astype(bf16)
    right_copy(0).start()
    if left_hops > 0:
        l_send[0] = own_sum((z + nz - left_hops) % nz).astype(bf16)
        left_copy(0).start()
    more_blocks(0)

    def step(s, _):
        right_copy(s - 1).wait_recv()
        total = own_sum((z + right_hops - s) % nz) + r_recv[s - 1].astype(f32)
        r_send[s] = total.astype(bf16)
        right_copy(s).start()

        @pl.when(s < left_hops)
        def _():
            left_copy(s - 1).wait_recv()
            other = own_sum((z + nz - left_hops + s) % nz) + l_recv[s - 1].astype(f32)
            l_send[s] = other.astype(bf16)
            left_copy(s).start()

        more_blocks(s)
        return 0

    half = max(right_hops // 2, 1)
    lax.fori_loop(1, half, step, 0)

    whole_wait(kv_recv.at[pl.ds(0, per_class)], kv_r)
    share = pl.ds(y * per_class, per_class)
    forwards = [
        pltpu.make_async_remote_copy(
            kv_recv.at[share],
            kv_recv.at[share],
            yf_s.at[t - 1],
            yf_r.at[t - 1],
            device_id=(me, group * SHARE + (y + t) % SHARE),
            device_id_type=MESH,
        )
        for t in range(1, SHARE)
    ]
    for forward in forwards:
        forward.start()

    lax.fori_loop(half, right_hops, step, 0)

    right_copy(right_hops - 1).wait_recv()
    total = own_sum(z) + r_recv[right_hops - 1].astype(f32)
    if left_hops > 0:
        left_copy(left_hops - 1).wait_recv()
        total = total + l_recv[left_hops - 1].astype(f32)
    wg_ref[...] = total

    for forward in forwards:
        forward.wait()

    def unpack_kv(i, _):
        parts = []
        for b in range(2):
            source = dst_ref[0, 2 * i + b]
            parts.append(kv_recv[kv_slot(source, me)])
        at = pl.ds(pl.multiple_of(2 * BR * i, 2 * BR), 2 * BR)
        for j in range(2):
            m_kv[j, at, :] = jnp.concatenate([part[BR * j : BR * (j + 1)] for part in parts], axis=0)
        return 0

    lax.fori_loop(0, n // 2, unpack_kv, 0)

    whole_wait(st_recv, st_r)
    whole_wait(qd_recv, qd_r)

    def unpack(i, _):
        parts = []
        for b in range(2):
            source = dst_ref[0, 2 * i + b]
            st_rows[pl.ds(2 * i + b, 1), :] = st_recv[source]
            parts.append(qd_recv[source])
        at = pl.ds(pl.multiple_of(2 * BR * i, 2 * BR), 2 * BR)
        for h in range(HPD):
            m_q[h, at, :] = jnp.concatenate([part[BR * h : BR * (h + 1)] for part in parts], axis=0)
            low = BR * (HPD + h)
            m_do[h, at, :] = jnp.concatenate([part[low : low + BR] for part in parts], axis=0)
        return 0

    lax.fori_loop(0, n // 2, unpack, 0)

    arrived = st_rows[...]
    st_cols[pl.ds(0, n, stride=BR), :] = arrived
    for r in range(1, BR):
        st_cols[pl.ds(r, n, stride=BR), :] = pltpu.roll(arrived, HD - 4 * r, 1)
    stats = st_cols[...].T[0:8]

    def segments(positions):
        end = len_ref[0, 0]
        found = (positions >= end).astype(jnp.int32)
        for j in range(1, len_ref.shape[1]):
            end = end + len_ref[0, j]
            found = found + (positions >= end).astype(jnp.int32)
        return found

    factor = HD ** (-0.5)
    nt = (((1,), (1,)), ((), ()))
    tn = (((0,), (0,)), ((), ()))
    dkv[...] = jnp.zeros_like(dkv)
    half_rows = rows // 2
    for part in range(2):
        low, high = part * half_rows, (part + 1) * half_rows
        k_pos = lax.broadcasted_iota(jnp.int32, (high, 1), 0)
        q_pos = lax.broadcasted_iota(jnp.int32, (1, half_rows), 1) + low
        allowed = (segments(k_pos) == segments(q_pos)) & (k_pos <= q_pos)
        k_head = m_kv[0, 0:high, :]
        v_head = m_kv[1, 0:high, :]
        for h in range(HPD):
            q_head = m_q[h, low:high, :]
            do_head = m_do[h, low:high, :]
            scores = lax.dot_general(k_head, q_head, nt, preferred_element_type=f32) * factor
            probs = jnp.where(allowed, jnp.exp(scores - stats[h : h + 1, low:high]), 0.0)
            dkv[0:high, HD:] += jnp.dot(probs.astype(bf16), do_head, preferred_element_type=f32)
            dprobs = lax.dot_general(v_head, do_head, nt, preferred_element_type=f32)
            delta = stats[HPD + h : HPD + h + 1, low:high]
            dscores = (probs * (dprobs - delta) * factor).astype(bf16)
            dkv[0:high, :HD] += jnp.dot(dscores, q_head, preferred_element_type=f32)
            q_grad = lax.dot_general(dscores, k_head, tn, preferred_element_type=f32)
            qg_ref[low:high, HD * h : HD * (h + 1)] = q_grad.astype(bf16)

    kept = rows // nm
    g_send[...] = dkv[...].astype(bf16).reshape(nm, kept, 2 * HD)
    pltpu.make_async_copy(g_send.at[mp], g_recv.at[mp], g_r).start()

    def send_grad(k, _):
        other = (mp + k) % nm
        pltpu.make_async_remote_copy(
            g_send.at[other], g_recv.at[mp], g_s, g_r, device_id=(me, other), device_id_type=MESH
        ).start()
        return 0

    lax.fori_loop(1, nm, send_grad, 0)

    whole_wait(qd_send.at[pl.ds(0, n - 1)], qd_s)
    whole_wait(st_send.at[pl.ds(0, n - 1)], st_s)

    @pl.when(has_self)
    def _():
        whole_wait(kv_send.at[pl.ds(0, per_class - 1)], kv_s)

    @pl.when(jnp.logical_not(has_self))
    def _():
        whole_wait(kv_send.at[pl.ds(0, per_class)], kv_s)

    def ring_sent(s, _):
        right_copy(s).wait_send()

        @pl.when(s < left_hops)
        def _():
            left_copy(s).wait_send()

        return 0

    lax.fori_loop(0, right_hops, ring_sent, 0)

    whole_wait(g_recv, g_r)
    groups = nm // SHARE
    for x in range(groups):
        total = g_recv[SHARE * x].astype(f32)
        for j in range(1, SHARE):
            total = total + g_recv[SHARE * x + j].astype(f32)
        total = total.astype(bf16)
        kvg_ref[:, HD * x : HD * (x + 1)] = total[:, :HD]
        kvg_ref[:, HD * (groups + x) : HD * (groups + x + 1)] = total[:, HD:]
    whole_wait(g_send.at[pl.ds(0, nm - 1)], g_s)


def body(
    queries,
    keys,
    values,
    attn_out,
    out_grad,
    lse,
    layer_grad,
    feedback,
    doc_lengths,
    src_order,
    dst_order,
):
    n, nm = lax.axis_size("dp"), lax.axis_size("mp")
    rows, cols = queries.shape
    nz = n // 2
    right_hops, left_hops = nz // 2, max(nz // 2 - 1, 1)
    kept = rows // nm
    owned = layer_grad.shape[1] // n
    f32, bf16 = jnp.float32, jnp.bfloat16
    smem = pl.BlockSpec(memory_space=pltpu.SMEM)
    vmem = pl.BlockSpec(memory_space=pltpu.VMEM)
    hbm = pl.BlockSpec(memory_space=pl.ANY)
    dma = pltpu.SemaphoreType.DMA

    def blocks(array):
        return array.reshape(n, BR, array.shape[1])

    return pl.pallas_call(
        functools.partial(kernel, n, nm),
        out_shape=(
            jax.ShapeDtypeStruct((rows, cols), bf16),
            jax.ShapeDtypeStruct((kept, 2 * keys.shape[1]), bf16),
            jax.ShapeDtypeStruct((owned, cols), f32),
        ),
        in_specs=[smem] * 3 + [vmem] * 5 + [hbm] * 4,
        out_specs=(vmem, vmem, vmem),
        scratch_shapes=[
            pltpu.VMEM((2, n, BR, HD), bf16),
            pltpu.VMEM(layer_grad.shape, bf16),
            pltpu.VMEM(feedback.shape[1:], bf16),
            pltpu.VMEM((rows, HD), f32),
            pltpu.VMEM((n, HD), f32),
            pltpu.VMEM((n, 4 * BR, HD), bf16),
            pltpu.VMEM((n, 4 * BR, HD), bf16),
            pltpu.VMEM((n, 2 * BR, HD), bf16),
            pltpu.VMEM((n, 2 * BR, HD), bf16),
            pltpu.VMEM((n, 1, HD), f32),
            pltpu.VMEM((n, 1, HD), f32),
            pltpu.VMEM((nz, owned, cols), f32),
            pltpu.VMEM((nz, owned, cols), bf16),
            pltpu.VMEM((nz, owned, cols), bf16),
            pltpu.VMEM((right_hops, owned, cols), bf16),
            pltpu.VMEM((right_hops, owned, cols), bf16),
            pltpu.VMEM((left_hops, owned, cols), bf16),
            pltpu.VMEM((left_hops, owned, cols), bf16),
            pltpu.VMEM((HPD, rows, HD), bf16),
            pltpu.VMEM((HPD, rows, HD), bf16),
            pltpu.VMEM((2, rows, HD), bf16),
            pltpu.VMEM((rows, 2 * HD), f32),
            pltpu.VMEM((nm, kept, 2 * HD), bf16),
            pltpu.VMEM((nm, kept, 2 * HD), bf16),
            dma((4,)),
            dma,
            dma,
            dma,
            dma,
            dma,
            dma,
            dma((SHARE - 1,)),
            dma((SHARE - 1,)),
            dma((nz // 2,)),
            dma((nz // 2,)),
            dma((right_hops,)),
            dma((right_hops,)),
            dma((left_hops,)),
            dma((left_hops,)),
            dma,
            dma,
        ],
        compiler_params=pltpu.CompilerParams(
            collective_id=0, has_side_effects=True, vmem_limit_bytes=48 * 1024 * 1024
        ),
    )(
        src_order,
        dst_order,
        doc_lengths,
        blocks(queries),
        blocks(out_grad),
        blocks(attn_out),
        attn_out,
        lse.astype(f32),
        blocks(keys),
        blocks(values),
        layer_grad,
        feedback[0],
    )


def solution(mesh):
    return jax.shard_map(
        body,
        mesh=mesh,
        in_specs=(
            P("dp", "mp"),
            P("dp", None),
            P("dp", None),
            P("dp", "mp"),
            P("dp", "mp"),
            P("dp", "mp"),
            P("dp", None),
            P("dp", None, "mp"),
            P("dp", None),
            P("dp", None),
            P("dp", None),
        ),
        out_specs=(P("dp", "mp"), P(("dp", "mp"), None), P("dp", "mp")),
        check_vma=False,
    )
```

time: 565 us -> 140 us (0.25)
  waiting for transfers between devices: 376 us -> 0 us
  Pallas kernels: 0 us -> 127 us
  blocking collectives: 93.5 us -> 0 us
  starting transfers between devices: 43 us -> 0 us
  between operations: 14.4 us -> 0.66 us
  other arithmetic: 13.1 us -> 0 us
  matrix products: 8.86 us -> 0 us
    reduce_scatter x2 -> x0, waiting for transfers between devices: 292 us -> none  [the longest x1 215 us: body(): lax.psum_scatter((levels.astype(jnp.float32) * scales.astype(jnp.float32)...]
    pallas_call x0 -> x1, Pallas kernels: none -> 127 us  [body(): pl.pallas_call(functools.partial(kernel, n, nm), out_shape=(jax.ShapeDtyp...]
    all_to_all x2 -> x0, blocking collectives: 93.5 us -> none  [the longest x1 47.1 us: body(): lax.all_to_all(to_blocks(queries), 'dp', split_axis=0, concat_axis=0, til...]
    all_to_all x3 -> x0, waiting for transfers between devices: 84.3 us -> none  [the longest x1 38 us: body(): lax.all_to_all(to_blocks(kv_pair), 'dp', split_axis=0, concat_axis=0, til...]
    all_to_all x3 -> x0, starting transfers between devices: 42.8 us -> none  [the longest x1 30.4 us: body(): lax.all_to_all(to_blocks(loader_delta), 'dp', split_axis=0, concat_axis=0...]
    dot_general x6 -> x0, matrix products: 8.86 us -> none  [the longest x1 6.54 us: body(): jnp.einsum('td,tc->dc', layer_grad, attn_out, preferred_element_type=jnp....]
    unnamed x23 -> x21, local copies, waits for them, and re-layouts: 3.42 us -> 10.4 us
    gather x10 -> x0, local copies, waits for them, and re-layouts: 6.21 us -> none  [the longest x5 3.11 us: to_blocks(): jnp.take(array.reshape(replicas, block_rows, array.shape[1]), send_order,...]
  transfers between devices with their start and end apart: 5 -> 0, of which waited for: 5 -> 0; matrix products, arithmetic and copies ran while one was open for 4% -> 0% of each run, Pallas kernels for 0% -> 0%
where the time goes in v1:
time: 140 us; the launch traced here: 139 us
  Pallas kernels  127 us (91%)
  local copies, waits for them, and re-layouts  11.3 us (8%)
    pallas_call x1, Pallas kernels, body(): pl.pallas_call(functools.partial(kernel, n, nm), out_shape=(jax.ShapeDtyp...  127 us
    unnamed x21, local copies, waits for them, and re-layouts  10.4 us

profile of v1, /device:TPU:1, one launch (start us, length us, event | category | flops | bytes accessed | tf_op | source)
XLA Modules:
  0.0 139.1 jit_solution(1713934333035633437)
XLA Ops:
  0.6 0.8 copy.15.lse_ref
  1.5 0.0 copy-start
  1.5 1.6 %copy-done = bf16[1,4096,256]{2,1,0:T(8,128)(2,1)S(1)} copy-done((bf16[1,4096,256]{2,1,0:T(8,128)(2,1)S(1)}, bf16[1,4096,256]{2,1,0:T(8,128)(2,1)}, u32[]{:S(2)}) %copy-start) | copy-done | bytes 2097176
  3.1 0.0 copy-start.1
  3.1 0.9 copy-done.1
  4.0 0.0 copy-start.2
  4.0 1.0 copy-done.2
  5.1 0.0 copy-start.3
  5.1 1.0 copy-done.3
  6.1 0.0 copy-start.4
  6.1 0.9 copy-done.4
  7.0 0.0 copy-start.5
  7.0 0.9 copy-done.5
  8.0 0.0 copy-start.6
  8.0 0.7 copy-done.6
  8.7 0.0 copy-start.7
  8.7 0.7 copy-done.7
  9.3 0.0 copy-start.8
  9.3 0.7 copy-done.8
  10.0 127.2 %shard_map.130 = (bf16[512,256]{1,0:T(8,128)(2,1)S(1)}, bf16[32,1024]{1,0:T(8,128)(2,1)S(1)}, f32[64,256]{1,0:T(8,128)S(1)}) custom-call(s32[1,64]{1,0:T(1,128)S(1)} %copy-done.6, s32[1,64]{1,0:T(1,128)S(1)} %copy-done.7, s32[1,8]{1,0:T(1,128)S(1)} %copy-done.8, bf16[64,8,256]{2,1,0:T(8,128)(2,1)S(1)} %bitcast.10, bf16[64,8,256]{2,1,0:T(8,128)(2,1)S(1)} %bitcast.11, ...), custom_call_target="tpu_custom_call" | custom-call | tf_op jit(solution)/shard_map/pallas_call | solution.py:463
  137.2 0.7 copy.19
  137.9 0.6 copy.20
  138.5 0.6 copy.21
Async XLA Ops:
  1.5 1.6 %copy-start = (bf16[1,4096,256]{2,1,0:T(8,128)(2,1)S(1)}, bf16[1,4096,256]{2,1,0:T(8,128)(2,1)}, u32[]{:S(2)}) copy-start(bf16[1,4096,256]{2,1,0:T(8,128)(2,1)} %param.18) | copy-start | bytes 6291460
  3.1 0.9 copy-start.1
  4.0 1.0 copy-start.2
  5.1 1.0 copy-start.3
  6.1 0.9 copy-start.4
  7.0 0.9 copy-start.5
  8.0 0.7 copy-start.6
  8.7 0.7 copy-start.7
  9.3 0.7 copy-start.8

commit v2 on v1

--- a/solution.py
+++ b/solution.py
@@ -14,7 +14,11 @@
 BR = 8
 SHARE = GROUP // HPD
 STRIDE = 29
-FIRST = 16
+SPAN = 2
+FIRST = 8
+PER = 8
+BEFORE = 7
+PASS = 4
 MESH = pl.DeviceIdType.MESH
 
 
@@ -25,14 +29,13 @@
 def kernel(
     n,
     nm,
-    src_ref,
-    dst_ref,
-    len_ref,
-    q_ref,
-    do_ref,
-    o3_ref,
-    o_ref,
-    lse_ref,
+    src_hbm,
+    dst_hbm,
+    len_hbm,
+    q_hbm,
+    do_hbm,
+    o_hbm,
+    lse_hbm,
     k_hbm,
     v_hbm,
     lg_hbm,
@@ -40,6 +43,16 @@
     qg_ref,
     kvg_ref,
     wg_ref,
+    qg_out,
+    kvg_out,
+    wg_out,
+    src_ref,
+    dst_ref,
+    len_ref,
+    q_ref,
+    do_ref,
+    o_ref,
+    lse_ref,
     kv_in,
     lg_v,
     fb_v,
@@ -54,10 +67,14 @@
     own,
     p_send,
     p_recv,
-    r_send,
-    r_recv,
-    l_send,
-    l_recv,
+    rc_send,
+    rc_recv,
+    rj_send,
+    rj_recv,
+    lc_send,
+    lc_recv,
+    lj_send,
+    lj_recv,
     m_q,
     m_do,
     m_kv,
@@ -75,10 +92,14 @@
     yf_r,
     p_s,
     p_r,
-    r_s,
-    r_r,
-    l_s,
-    l_r,
+    rc_s,
+    rc_r,
+    rj_s,
+    rj_r,
+    lc_s,
+    lc_r,
+    lj_s,
+    lj_r,
     g_s,
     g_r,
 ):
@@ -89,18 +110,25 @@
     z, core = me // 2, me % 2
     nz = n // 2
     rows = n * BR
-    right_hops, left_hops = nz // 2, nz // 2 - 1
     per_class = n // SHARE
 
     column = pl.ds(pl.multiple_of(group * HD, HD), HD)
-    k_copy = pltpu.make_async_copy(k_hbm.at[:, :, column], kv_in.at[0], loc_sem.at[0])
-    v_copy = pltpu.make_async_copy(v_hbm.at[:, :, column], kv_in.at[1], loc_sem.at[1])
-    lg_copy = pltpu.make_async_copy(lg_hbm, lg_v, loc_sem.at[2])
-    fb_copy = pltpu.make_async_copy(fb_hbm, fb_v, loc_sem.at[3])
-    k_copy.start()
-    v_copy.start()
-    lg_copy.start()
-    fb_copy.start()
+    loads = [
+        (do_hbm, do_ref),
+        (o_hbm, o_ref),
+        (lse_hbm, lse_ref),
+        (src_hbm, src_ref),
+        (q_hbm, q_ref),
+        (k_hbm.at[:, :, column], kv_in.at[0]),
+        (v_hbm.at[:, :, column], kv_in.at[1]),
+        (dst_hbm, dst_ref),
+        (len_hbm, len_ref),
+        (lg_hbm, lg_v),
+        (fb_hbm, fb_v),
+    ]
+    loads = [pltpu.make_async_copy(a, b, loc_sem.at[i]) for i, (a, b) in enumerate(loads)]
+    for load in loads:
+        load.start()
 
     barrier = pltpu.get_barrier_semaphore()
 
@@ -115,50 +143,36 @@
     lax.fori_loop(1, n, greet_dp, 0)
     lax.fori_loop(1, nm, greet_mp, 0)
 
-    product = (do_ref[...].astype(f32) * o3_ref[...].astype(f32)).reshape(rows, HPD * HD)
+    for load in loads[:3]:
+        load.wait()
+    product = do_ref[...].astype(f32).reshape(rows, HPD * HD) * o_ref[...].astype(f32)
     delta0 = jnp.sum(product[:, :HD], axis=1, keepdims=True)
     delta1 = jnp.sum(product[:, HD:], axis=1, keepdims=True)
-    lse = lse_ref[...]
+    lse = jnp.concatenate(
+        [lse_ref[...].astype(f32), jnp.zeros((HD - HPD, rows), f32)], axis=0
+    ).T
     lane = lax.broadcasted_iota(jnp.int32, (rows, HD), 1)
-    st_cols[...] = jnp.where(
-        lane == 0,
-        lse[:, 0:1],
-        jnp.where(
-            lane == 1,
-            lse[:, 1:2],
-            jnp.where(lane == 2, delta0, jnp.where(lane == 3, delta1, 0.0)),
-        ),
-    )
+    st_cols[...] = jnp.where(lane == 2, delta0, jnp.where(lane == 3, delta1, lse))
     packed = st_cols[pl.ds(0, n, stride=BR), :]
     for r in range(1, BR):
         packed = packed + pltpu.roll(st_cols[pl.ds(r, n, stride=BR), :], 4 * r, 1)
     st_rows[...] = packed
 
-    k_copy.wait()
-    v_copy.wait()
-
-    def pack(d, _):
-        block = src_ref[0, d]
-        kv_send[d] = jnp.concatenate([kv_in[0, block], kv_in[1, block]], axis=0)
-        st_send[d] = st_rows[pl.ds(block, 1), :]
-        qb = q_ref[block]
-        db = do_ref[block]
-        qd_send[d] = jnp.concatenate([qb[:, :HD], qb[:, HD:], db[:, :HD], db[:, HD:]], axis=0)
-        return 0
-
-    lax.fori_loop(0, n, pack, 0)
+    for load in loads[3:7]:
+        load.wait()
 
     pl.semaphore_wait(barrier, n - 1 + nm - 1)
 
     def kv_slot(source, dest):
         return ((source + dest) % SHARE) * per_class + source // SHARE
 
-    own_slot = kv_slot(me, me)
     has_self = (me + me) % SHARE == y
 
     def send_kv(j, _):
         d = SHARE * ((me // SHARE + j) % per_class) + (y + SHARE - me % SHARE) % SHARE
         slot = y * per_class + me // SHARE
+        block = src_ref[0, d]
+        kv_send[d] = jnp.concatenate([kv_in[0, block], kv_in[1, block]], axis=0)
 
         @pl.when(d == me)
         def _():
@@ -174,11 +188,20 @@
 
     lax.fori_loop(0, per_class, send_kv, 0)
 
+    def pack(d):
+        block = src_ref[0, d]
+        st_send[d] = st_rows[pl.ds(block, 1), :]
+        qb = q_ref[block]
+        db = do_ref[block]
+        qd_send[d] = jnp.concatenate([qb[:, :HD], qb[:, HD:], db[:, :HD], db[:, HD:]], axis=0)
+
+    pack(me)
     pltpu.make_async_copy(qd_send.at[me], qd_recv.at[me], qd_r).start()
     pltpu.make_async_copy(st_send.at[me], st_recv.at[me], st_r).start()
 
     def send_block(t, _):
         d = (me + t * STRIDE) % n
+        pack(d)
         pltpu.make_async_remote_copy(
             qd_send.at[d], qd_recv.at[me], qd_s, qd_r, device_id=(d, mp), device_id_type=MESH
         ).start()
@@ -189,10 +212,9 @@
 
     first = min(FIRST, n)
     lax.fori_loop(1, first, send_block, 0)
-    per_step = -(-(n - first) // right_hops)
-
-    lg_copy.wait()
-    fb_copy.wait()
+
+    for load in loads[7:]:
+        load.wait()
     partner = me + 1 - 2 * core
 
     def partner_copy(g):
@@ -234,59 +256,93 @@
 
     lax.fori_loop(0, nz // 2, partner_wait, 0)
 
-    def right_copy(s):
+    sides = (
+        (1, nz // 2, rc_send, rc_recv, rj_send, rj_recv, rc_s, rc_r, rj_s, rj_r),
+        (-1, nz // 2 - 1, lc_send, lc_recv, lj_send, lj_recv, lc_s, lc_r, lj_s, lj_r),
+    )
+
+    def chip_at(distance):
+        return (z + distance % nz) % nz
+
+    def device_at(distance):
+        return (chip_at(distance) * 2 + core, mp)
+
+    def own_sum(distance):
+        chip = chip_at(distance)
+        return own[chip] + p_recv[chip].astype(f32)
+
+    def walk_count(limit, j):
+        return len([k for k in range(nz) if SPAN * k + j <= limit])
+
+    def walk_copy(side, t):
+        sign, limit, send, recv, _, _, s_sem, r_sem, _, _ = side
+        part = pl.ds(0, walk_count(limit, SPAN - t))
         return pltpu.make_async_remote_copy(
-            r_send.at[s],
-            r_recv.at[s],
-            r_s.at[s],
-            r_r.at[s],
-            device_id=(((z + 1) % nz) * 2 + core, mp),
+            send.at[t, part],
+            recv.at[t, part],
+            s_sem.at[t],
+            r_sem.at[t],
+            device_id=device_at(sign),
             device_id_type=MESH,
         )
 
-    def left_copy(s):
+    def jump_copy(side, u):
+        sign, limit, _, _, send, recv, _, _, s_sem, r_sem = side
+        last = u == walk_count(limit, 1) - 1
         return pltpu.make_async_remote_copy(
-            l_send.at[s],
-            l_recv.at[s],
-            l_s.at[s],
-            l_r.at[s],
-            device_id=(((z + nz - 1) % nz) * 2 + core, mp),
+            send.at[u],
+            recv.at[u],
+            s_sem.at[u],
+            r_sem.at[u],
+            device_id=device_at(sign if last else sign * SPAN),
             device_id_type=MESH,
         )
 
-    def own_sum(chip):
-        return own[chip] + p_recv[chip].astype(f32)
-
-    def more_blocks(s):
-        begin = jnp.minimum(first + s * per_step, n)
-        end = jnp.minimum(begin + per_step, n)
-        lax.fori_loop(begin, end, send_block, 0)
-
-    r_send[0] = own_sum((z + right_hops) % nz).astype(bf16)
-    right_copy(0).start()
-    if left_hops > 0:
-        l_send[0] = own_sum((z + nz - left_hops) % nz).astype(bf16)
-        left_copy(0).start()
-    more_blocks(0)
-
-    def step(s, _):
-        right_copy(s - 1).wait_recv()
-        total = own_sum((z + right_hops - s) % nz) + r_recv[s - 1].astype(f32)
-        r_send[s] = total.astype(bf16)
-        right_copy(s).start()
-
-        @pl.when(s < left_hops)
-        def _():
-            left_copy(s - 1).wait_recv()
-            other = own_sum((z + nz - left_hops + s) % nz) + l_recv[s - 1].astype(f32)
-            l_send[s] = other.astype(bf16)
-            left_copy(s).start()
-
-        more_blocks(s)
-        return 0
-
-    half = max(right_hops // 2, 1)
-    lax.fori_loop(1, half, step, 0)
+    def walk(side, t):
+        sign, limit, send, recv = side[:4]
+        j = SPAN - t
+        came = walk_count(limit, j + 1) if t > 0 else 0
+        if came:
+            walk_copy(side, t - 1).wait_recv()
+        for k in range(walk_count(limit, j)):
+            total = own_sum(sign * (SPAN * k + j))
+            if k < came:
+                total = total + recv[t - 1, k].astype(f32)
+            send[t, k] = total.astype(bf16)
+        if walk_count(limit, j):
+            walk_copy(side, t).start()
+
+    def jump(side, u):
+        sign, limit, _, walked, send, recv = side[:6]
+        k = walk_count(limit, 1) - 1 - u
+        if k < 0:
+            return
+        came = walk_count(limit, 2)
+        if u == 0 and came:
+            walk_copy(side, SPAN - 2).wait_recv()
+        total = own_sum(sign * (SPAN * k + 1))
+        if k < came:
+            total = total + walked[SPAN - 2, k].astype(f32)
+        if u > 0:
+            jump_copy(side, u - 1).wait_recv()
+            total = total + recv[u - 1].astype(f32)
+        send[u] = total.astype(bf16)
+        jump_copy(side, u).start()
+
+    jumps = walk_count(nz // 2, 1)
+    stage_count = SPAN - 1 + jumps
+    before = min(BEFORE, stage_count)
+
+    def stage(i):
+        for side in sides:
+            if i < SPAN - 1:
+                walk(side, i)
+            else:
+                jump(side, i - (SPAN - 1))
+
+    for i in range(min(PASS, before)):
+        stage(i)
+        lax.fori_loop(min(first + i * PER, n), min(first + (i + 1) * PER, n), send_block, 0)
 
     whole_wait(kv_recv.at[pl.ds(0, per_class)], kv_r)
     share = pl.ds(y * per_class, per_class)
@@ -304,14 +360,10 @@
     for forward in forwards:
         forward.start()
 
-    lax.fori_loop(half, right_hops, step, 0)
-
-    right_copy(right_hops - 1).wait_recv()
-    total = own_sum(z) + r_recv[right_hops - 1].astype(f32)
-    if left_hops > 0:
-        left_copy(left_hops - 1).wait_recv()
-        total = total + l_recv[left_hops - 1].astype(f32)
-    wg_ref[...] = total
+    for i in range(min(PASS, before), before):
+        stage(i)
+        lax.fori_loop(min(first + i * PER, n), min(first + (i + 1) * PER, n), send_block, 0)
+    lax.fori_loop(min(first + before * PER, n), n, send_block, 0)
 
     for forward in forwards:
         forward.wait()
@@ -383,7 +435,10 @@
             dscores = (probs * (dprobs - delta) * factor).astype(bf16)
             dkv[0:high, :HD] += jnp.dot(dscores, q_head, preferred_element_type=f32)
             q_grad = lax.dot_general(dscores, k_head, tn, preferred_element_type=f32)
-            qg_ref[low:high, HD * h : HD * (h + 1)] = q_grad.astype(bf16)
+            qg_out[low:high, HD * h : HD * (h + 1)] = q_grad.astype(bf16)
+
+    qg_store = pltpu.make_async_copy(qg_out, qg_ref, loc_sem.at[0])
+    qg_store.start()
 
     kept = rows // nm
     g_send[...] = dkv[...].astype(bf16).reshape(nm, kept, 2 * HD)
@@ -398,6 +453,18 @@
 
     lax.fori_loop(1, nm, send_grad, 0)
 
+    for i in range(before, stage_count):
+        stage(i)
+    total = own_sum(0)
+    for side in sides:
+        count = walk_count(side[1], 1)
+        if count:
+            jump_copy(side, count - 1).wait_recv()
+            total = total + side[5][count - 1].astype(f32)
+    wg_out[...] = total
+    wg_store = pltpu.make_async_copy(wg_out, wg_ref, loc_sem.at[1])
+    wg_store.start()
+
     whole_wait(qd_send.at[pl.ds(0, n - 1)], qd_s)
     whole_wait(st_send.at[pl.ds(0, n - 1)], st_s)
 
@@ -409,16 +476,12 @@
     def _():
         whole_wait(kv_send.at[pl.ds(0, per_class)], kv_s)
 
-    def ring_sent(s, _):
-        right_copy(s).wait_send()
-
-        @pl.when(s < left_hops)
-        def _():
-            left_copy(s).wait_send()
-
-        return 0
-
-    lax.fori_loop(0, right_hops, ring_sent, 0)
+    for side in sides:
+        for t in range(SPAN - 1):
+            if walk_count(side[1], SPAN - t):
+                walk_copy(side, t).wait_send()
+        for u in range(walk_count(side[1], 1)):
+            jump_copy(side, u).wait_send()
 
     whole_wait(g_recv, g_r)
     groups = nm // SHARE
@@ -427,9 +490,14 @@
         for j in range(1, SHARE):
             total = total + g_recv[SHARE * x + j].astype(f32)
         total = total.astype(bf16)
-        kvg_ref[:, HD * x : HD * (x + 1)] = total[:, :HD]
-        kvg_ref[:, HD * (groups + x) : HD * (groups + x + 1)] = total[:, HD:]
+        kvg_out[:, HD * x : HD * (x + 1)] = total[:, :HD]
+        kvg_out[:, HD * (groups + x) : HD * (groups + x + 1)] = total[:, HD:]
+    kvg_store = pltpu.make_async_copy(kvg_out, kvg_ref, loc_sem.at[2])
+    kvg_store.start()
     whole_wait(g_send.at[pl.ds(0, nm - 1)], g_s)
+    qg_store.wait()
+    wg_store.wait()
+    kvg_store.wait()
 
 
 def body(
@@ -448,28 +516,38 @@
     n, nm = lax.axis_size("dp"), lax.axis_size("mp")
     rows, cols = queries.shape
     nz = n // 2
-    right_hops, left_hops = nz // 2, max(nz // 2 - 1, 1)
+    jumps = -(-(nz // 2) // SPAN)
     kept = rows // nm
     owned = layer_grad.shape[1] // n
     f32, bf16 = jnp.float32, jnp.bfloat16
-    smem = pl.BlockSpec(memory_space=pltpu.SMEM)
-    vmem = pl.BlockSpec(memory_space=pltpu.VMEM)
-    hbm = pl.BlockSpec(memory_space=pl.ANY)
+    hbm = pl.BlockSpec(memory_space=pltpu.HBM)
     dma = pltpu.SemaphoreType.DMA
+    walks = [pltpu.VMEM((SPAN - 1, jumps, owned, cols), bf16)] * 2
+    walks += [pltpu.VMEM((jumps, owned, cols), bf16)] * 2
+    walk_sems = [dma((SPAN - 1,))] * 2 + [dma((jumps,))] * 2
 
     def blocks(array):
         return array.reshape(n, BR, array.shape[1])
 
+    outs = (
+        jax.ShapeDtypeStruct((rows, cols), bf16),
+        jax.ShapeDtypeStruct((kept, 2 * keys.shape[1]), bf16),
+        jax.ShapeDtypeStruct((owned, cols), f32),
+    )
     return pl.pallas_call(
         functools.partial(kernel, n, nm),
-        out_shape=(
-            jax.ShapeDtypeStruct((rows, cols), bf16),
-            jax.ShapeDtypeStruct((kept, 2 * keys.shape[1]), bf16),
-            jax.ShapeDtypeStruct((owned, cols), f32),
-        ),
-        in_specs=[smem] * 3 + [vmem] * 5 + [hbm] * 4,
-        out_specs=(vmem, vmem, vmem),
+        out_shape=outs,
+        in_specs=[hbm] * 11,
+        out_specs=(hbm, hbm, hbm),
         scratch_shapes=[
+            *(pltpu.VMEM(out.shape, out.dtype) for out in outs),
+            pltpu.SMEM(src_order.shape, jnp.int32),
+            pltpu.SMEM(dst_order.shape, jnp.int32),
+            pltpu.SMEM(doc_lengths.shape, jnp.int32),
+            pltpu.VMEM((n, BR, cols), bf16),
+            pltpu.VMEM((n, BR, cols), bf16),
+            pltpu.VMEM((rows, cols), bf16),
+            pltpu.VMEM((HPD, rows), bf16),
             pltpu.VMEM((2, n, BR, HD), bf16),
             pltpu.VMEM(layer_grad.shape, bf16),
             pltpu.VMEM(feedback.shape[1:], bf16),
@@ -484,17 +562,15 @@
             pltpu.VMEM((nz, owned, cols), f32),
             pltpu.VMEM((nz, owned, cols), bf16),
             pltpu.VMEM((nz, owned, cols), bf16),
-            pltpu.VMEM((right_hops, owned, cols), bf16),
-            pltpu.VMEM((right_hops, owned, cols), bf16),
-            pltpu.VMEM((left_hops, owned, cols), bf16),
-            pltpu.VMEM((left_hops, owned, cols), bf16),
+            *walks,
+            *walks,
             pltpu.VMEM((HPD, rows, HD), bf16),
             pltpu.VMEM((HPD, rows, HD), bf16),
             pltpu.VMEM((2, rows, HD), bf16),
             pltpu.VMEM((rows, 2 * HD), f32),
             pltpu.VMEM((nm, kept, 2 * HD), bf16),
             pltpu.VMEM((nm, kept, 2 * HD), bf16),
-            dma((4,)),
+            dma((11,)),
             dma,
             dma,
             dma,
@@ -505,15 +581,13 @@
             dma((SHARE - 1,)),
             dma((nz // 2,)),
             dma((nz // 2,)),
-            dma((right_hops,)),
-            dma((right_hops,)),
-            dma((left_hops,)),
-            dma((left_hops,)),
+            *walk_sems,
+            *walk_sems,
             dma,
             dma,
         ],
         compiler_params=pltpu.CompilerParams(
-            collective_id=0, has_side_effects=True, vmem_limit_bytes=48 * 1024 * 1024
+            collective_id=0, has_side_effects=True, vmem_limit_bytes=60 * 1024 * 1024
         ),
     )(
         src_order,
@@ -521,9 +595,8 @@
         doc_lengths,
         blocks(queries),
         blocks(out_grad),
-        blocks(attn_out),
         attn_out,
-        lse.astype(f32),
+        lse.T,
         blocks(keys),
         blocks(values),
         layer_grad,

time: 140 us -> 120 us (0.86)
  Pallas kernels: 127 us -> 114 us
  local copies, waits for them, and re-layouts: 11.3 us -> 4.61 us
    pallas_call x1, Pallas kernels: 127 us -> 114 us  [body(): pl.pallas_call(functools.partial(kernel, n, nm), out_shape=outs, in_specs...]
    unnamed x21 -> x3, local copies, waits for them, and re-layouts: 10.4 us -> 4.61 us
where the time goes in v2:
time: 120 us
  Pallas kernels  114 us (95%)
  local copies, waits for them, and re-layouts  4.61 us (4%)
    pallas_call x1, Pallas kernels, body(): pl.pallas_call(functools.partial(kernel, n, nm), out_shape=outs, in_specs...  114 us
    unnamed x3, local copies, waits for them, and re-layouts  4.61 us

profile of v2, /device:TPU:1, one launch (start us, length us, event | category | flops | bytes accessed | tf_op | source)
XLA Modules:
  0.0 119.7 jit_solution(8240147125463126433)
XLA Ops:
  0.6 114.4 %shard_map.130 = (bf16[512,256]{1,0:T(8,128)(2,1)}, bf16[32,1024]{1,0:T(8,128)(2,1)}, f32[64,256]{1,0:T(8,128)}) custom-call(s32[1,64]{1,0:T(1,128)} %src_hbm.1, s32[1,64]{1,0:T(1,128)} %dst_hbm.1, s32[1,8]{1,0:T(1,128)} %len_hbm.1, bf16[64,8,256]{2,1,0:T(8,128)(2,1)} %bitcast.9, bf16[64,8,256]{2,1,0:T(8,128)(2,1)} %bitcast.10, bf16[512,256]{1,0:T(8,128)(2,1)} %o_hbm.1, ...), custom_call_target="tpu_custom_call" | custom-call | tf_op jit(solution)/shard_map/pallas_call | solution.py:537
  115.1 1.7 %copy.17 = bf16[512,256]{1,0:T(8,128)(2,1)} copy(bf16[512,256]{1,0:T(8,128)(2,1)} %get-tuple-element.6) | data formatting | bytes 524288
  116.8 1.5 %copy.18 = bf16[32,1024]{1,0:T(8,128)(2,1)} copy(bf16[32,1024]{1,0:T(8,128)(2,1)} %get-tuple-element.7) | data formatting | bytes 131072
  118.2 1.5 %copy.19 = f32[64,256]{1,0:T(8,128)} copy(f32[64,256]{1,0:T(8,128)} %get-tuple-element.8) | data formatting | bytes 131072

commit v3 on v2

--- a/solution.py
+++ b/solution.py
@@ -17,7 +17,7 @@
 SPAN = 2
 FIRST = 8
 PER = 8
-BEFORE = 7
+BEFORE = 8
 PASS = 4
 MESH = pl.DeviceIdType.MESH
 
@@ -29,9 +29,7 @@
 def kernel(
     n,
     nm,
-    src_hbm,
-    dst_hbm,
-    len_hbm,
+    order_hbm,
     q_hbm,
     do_hbm,
     o_hbm,
@@ -46,9 +44,7 @@
     qg_out,
     kvg_out,
     wg_out,
-    src_ref,
-    dst_ref,
-    len_ref,
+    order_ref,
     q_ref,
     do_ref,
     o_ref,
@@ -114,15 +110,13 @@
 
     column = pl.ds(pl.multiple_of(group * HD, HD), HD)
     loads = [
+        (order_hbm, order_ref),
+        (q_hbm, q_ref),
         (do_hbm, do_ref),
+        (k_hbm.at[:, :, column], kv_in.at[0]),
+        (v_hbm.at[:, :, column], kv_in.at[1]),
         (o_hbm, o_ref),
         (lse_hbm, lse_ref),
-        (src_hbm, src_ref),
-        (q_hbm, q_ref),
-        (k_hbm.at[:, :, column], kv_in.at[0]),
-        (v_hbm.at[:, :, column], kv_in.at[1]),
-        (dst_hbm, dst_ref),
-        (len_hbm, len_ref),
         (lg_hbm, lg_v),
         (fb_hbm, fb_v),
     ]
@@ -144,6 +138,75 @@
     lax.fori_loop(1, nm, greet_mp, 0)
 
     for load in loads[:3]:
+        load.wait()
+
+    pl.semaphore_wait(barrier, n - 1 + nm - 1)
+
+    def kv_slot(source, dest):
+        return ((source + dest) % SHARE) * per_class + source // SHARE
+
+    has_self = (me + me) % SHARE == y
+
+    def send_kv(j, _):
+        d = SHARE * ((me // SHARE + 7 * j) % per_class) + (y + SHARE - me % SHARE) % SHARE
+        slot = y * per_class + me // SHARE
+        block = order_ref[0, d]
+        kv_send[d] = jnp.concatenate([kv_in[0, block], kv_in[1, block]], axis=0)
+
+        @pl.when(d == me)
+        def _():
+            pltpu.make_async_copy(kv_send.at[me], kv_recv.at[slot], kv_r).start()
+
+        @pl.when(d != me)
+        def _():
+            pltpu.make_async_remote_copy(
+                kv_send.at[d], kv_recv.at[slot], kv_s, kv_r, device_id=(d, mp), device_id_type=MESH
+            ).start()
+
+        return 0
+
+
+    def pack(d):
+        block = order_ref[0, d]
+        qb = q_ref[block]
+        db = do_ref[block]
+        qd_send[d] = jnp.concatenate([qb[:, :HD], qb[:, HD:], db[:, :HD], db[:, HD:]], axis=0)
+
+    pack(me)
+    pltpu.make_async_copy(qd_send.at[me], qd_recv.at[me], qd_r).start()
+
+    def send_to(chip, other_core):
+        d = (z + chip + nz) % nz * 2 + (core + other_core) % 2
+        pack(d)
+        pltpu.make_async_remote_copy(
+            qd_send.at[d], qd_recv.at[me], qd_s, qd_r, device_id=(d, mp), device_id_type=MESH
+        ).start()
+
+    half = nz // 2
+    most = 4 * (half - 2)
+
+    def send_block(t, _):
+        pair, sub = t // 8, t % 8
+        near = sub // 2 % 2
+        distance = (1 - near) * (half - 1 - pair) + near * (1 + pair)
+        send_to((1 - 2 * (sub % 2)) * distance, sub // 4)
+        return 0
+
+    def send_middle(t, _):
+        send_to((1 - 2 * (t % 2)) * (half // 2), t // 2)
+        return 0
+
+    send_to(half, 0)
+    send_to(0, 1)
+    send_to(half, 1)
+    lax.fori_loop(0, 4, send_middle, 0)
+    first = min(FIRST, most)
+    lax.fori_loop(0, first, send_block, 0)
+    for load in loads[3:5]:
+        load.wait()
+    lax.fori_loop(0, per_class, send_kv, 0)
+
+    for load in loads[5:7]:
         load.wait()
     product = do_ref[...].astype(f32).reshape(rows, HPD * HD) * o_ref[...].astype(f32)
     delta0 = jnp.sum(product[:, :HD], axis=1, keepdims=True)
@@ -158,60 +221,17 @@
         packed = packed + pltpu.roll(st_cols[pl.ds(r, n, stride=BR), :], 4 * r, 1)
     st_rows[...] = packed
 
-    for load in loads[3:7]:
-        load.wait()
-
-    pl.semaphore_wait(barrier, n - 1 + nm - 1)
-
-    def kv_slot(source, dest):
-        return ((source + dest) % SHARE) * per_class + source // SHARE
-
-    has_self = (me + me) % SHARE == y
-
-    def send_kv(j, _):
-        d = SHARE * ((me // SHARE + j) % per_class) + (y + SHARE - me % SHARE) % SHARE
-        slot = y * per_class + me // SHARE
-        block = src_ref[0, d]
-        kv_send[d] = jnp.concatenate([kv_in[0, block], kv_in[1, block]], axis=0)
-
-        @pl.when(d == me)
-        def _():
-            pltpu.make_async_copy(kv_send.at[me], kv_recv.at[slot], kv_r).start()
-
-        @pl.when(d != me)
-        def _():
-            pltpu.make_async_remote_copy(
-                kv_send.at[d], kv_recv.at[slot], kv_s, kv_r, device_id=(d, mp), device_id_type=MESH
-            ).start()
-
-        return 0
-
-    lax.fori_loop(0, per_class, send_kv, 0)
-
-    def pack(d):
-        block = src_ref[0, d]
-        st_send[d] = st_rows[pl.ds(block, 1), :]
-        qb = q_ref[block]
-        db = do_ref[block]
-        qd_send[d] = jnp.concatenate([qb[:, :HD], qb[:, HD:], db[:, :HD], db[:, HD:]], axis=0)
-
-    pack(me)
-    pltpu.make_async_copy(qd_send.at[me], qd_recv.at[me], qd_r).start()
-    pltpu.make_async_copy(st_send.at[me], st_recv.at[me], st_r).start()
-
-    def send_block(t, _):
+    def send_stats(t, _):
         d = (me + t * STRIDE) % n
-        pack(d)
-        pltpu.make_async_remote_copy(
-            qd_send.at[d], qd_recv.at[me], qd_s, qd_r, device_id=(d, mp), device_id_type=MESH
-        ).start()
+        st_send[d] = st_rows[pl.ds(order_ref[0, d], 1), :]
         pltpu.make_async_remote_copy(
             st_send.at[d], st_recv.at[me], st_s, st_r, device_id=(d, mp), device_id_type=MESH
         ).start()
         return 0
 
-    first = min(FIRST, n)
-    lax.fori_loop(1, first, send_block, 0)
+    st_send[me] = st_rows[pl.ds(order_ref[0, me], 1), :]
+    pltpu.make_async_copy(st_send.at[me], st_recv.at[me], st_r).start()
+    lax.fori_loop(1, n, send_stats, 0)
 
     for load in loads[7:]:
         load.wait()
@@ -274,14 +294,13 @@
     def walk_count(limit, j):
         return len([k for k in range(nz) if SPAN * k + j <= limit])
 
-    def walk_copy(side, t):
-        sign, limit, send, recv, _, _, s_sem, r_sem, _, _ = side
-        part = pl.ds(0, walk_count(limit, SPAN - t))
+    def walk_copy(side, t, k):
+        sign, _, send, recv, _, _, s_sem, r_sem, _, _ = side
         return pltpu.make_async_remote_copy(
-            send.at[t, part],
-            recv.at[t, part],
-            s_sem.at[t],
-            r_sem.at[t],
+            send.at[t, k],
+            recv.at[t, k],
+            s_sem.at[t, k],
+            r_sem.at[t, k],
             device_id=device_at(sign),
             device_id_type=MESH,
         )
@@ -302,26 +321,22 @@
         sign, limit, send, recv = side[:4]
         j = SPAN - t
         came = walk_count(limit, j + 1) if t > 0 else 0
-        if came:
-            walk_copy(side, t - 1).wait_recv()
-        for k in range(walk_count(limit, j)):
+        for k in reversed(range(walk_count(limit, j))):
             total = own_sum(sign * (SPAN * k + j))
             if k < came:
+                walk_copy(side, t - 1, k).wait_recv()
                 total = total + recv[t - 1, k].astype(f32)
             send[t, k] = total.astype(bf16)
-        if walk_count(limit, j):
-            walk_copy(side, t).start()
+            walk_copy(side, t, k).start()
 
     def jump(side, u):
         sign, limit, _, walked, send, recv = side[:6]
         k = walk_count(limit, 1) - 1 - u
         if k < 0:
             return
-        came = walk_count(limit, 2)
-        if u == 0 and came:
-            walk_copy(side, SPAN - 2).wait_recv()
         total = own_sum(sign * (SPAN * k + 1))
-        if k < came:
+        if k < walk_count(limit, 2):
+            walk_copy(side, SPAN - 2, k).wait_recv()
             total = total + walked[SPAN - 2, k].astype(f32)
         if u > 0:
             jump_copy(side, u - 1).wait_recv()
@@ -342,7 +357,7 @@
 
     for i in range(min(PASS, before)):
         stage(i)
-        lax.fori_loop(min(first + i * PER, n), min(first + (i + 1) * PER, n), send_block, 0)
+        lax.fori_loop(min(first + i * PER, most), min(first + (i + 1) * PER, most), send_block, 0)
 
     whole_wait(kv_recv.at[pl.ds(0, per_class)], kv_r)
     share = pl.ds(y * per_class, per_class)
@@ -362,8 +377,8 @@
 
     for i in range(min(PASS, before), before):
         stage(i)
-        lax.fori_loop(min(first + i * PER, n), min(first + (i + 1) * PER, n), send_block, 0)
-    lax.fori_loop(min(first + before * PER, n), n, send_block, 0)
+        lax.fori_loop(min(first + i * PER, most), min(first + (i + 1) * PER, most), send_block, 0)
+    lax.fori_loop(min(first + before * PER, most), most, send_block, 0)
 
     for forward in forwards:
         forward.wait()
@@ -371,7 +386,7 @@
     def unpack_kv(i, _):
         parts = []
         for b in range(2):
-            source = dst_ref[0, 2 * i + b]
+            source = order_ref[0, n + 2 * i + b]
             parts.append(kv_recv[kv_slot(source, me)])
         at = pl.ds(pl.multiple_of(2 * BR * i, 2 * BR), 2 * BR)
         for j in range(2):
@@ -386,7 +401,7 @@
     def unpack(i, _):
         parts = []
         for b in range(2):
-            source = dst_ref[0, 2 * i + b]
+            source = order_ref[0, n + 2 * i + b]
             st_rows[pl.ds(2 * i + b, 1), :] = st_recv[source]
             parts.append(qd_recv[source])
         at = pl.ds(pl.multiple_of(2 * BR * i, 2 * BR), 2 * BR)
@@ -405,10 +420,10 @@
     stats = st_cols[...].T[0:8]
 
     def segments(positions):
-        end = len_ref[0, 0]
+        end = order_ref[0, 2 * n]
         found = (positions >= end).astype(jnp.int32)
-        for j in range(1, len_ref.shape[1]):
-            end = end + len_ref[0, j]
+        for j in range(1, order_ref.shape[1] - 2 * n):
+            end = end + order_ref[0, 2 * n + j]
             found = found + (positions >= end).astype(jnp.int32)
         return found
 
@@ -478,8 +493,8 @@
 
     for side in sides:
         for t in range(SPAN - 1):
-            if walk_count(side[1], SPAN - t):
-                walk_copy(side, t).wait_send()
+            for k in range(walk_count(side[1], SPAN - t)):
+                walk_copy(side, t, k).wait_send()
         for u in range(walk_count(side[1], 1)):
             jump_copy(side, u).wait_send()
 
@@ -524,11 +539,12 @@
     dma = pltpu.SemaphoreType.DMA
     walks = [pltpu.VMEM((SPAN - 1, jumps, owned, cols), bf16)] * 2
     walks += [pltpu.VMEM((jumps, owned, cols), bf16)] * 2
-    walk_sems = [dma((SPAN - 1,))] * 2 + [dma((jumps,))] * 2
+    walk_sems = [dma((SPAN - 1, jumps))] * 2 + [dma((jumps,))] * 2
 
     def blocks(array):
         return array.reshape(n, BR, array.shape[1])
 
+    order = jnp.concatenate([src_order, dst_order, doc_lengths], axis=1)
     outs = (
         jax.ShapeDtypeStruct((rows, cols), bf16),
         jax.ShapeDtypeStruct((kept, 2 * keys.shape[1]), bf16),
@@ -537,13 +553,11 @@
     return pl.pallas_call(
         functools.partial(kernel, n, nm),
         out_shape=outs,
-        in_specs=[hbm] * 11,
+        in_specs=[hbm] * 9,
         out_specs=(hbm, hbm, hbm),
         scratch_shapes=[
             *(pltpu.VMEM(out.shape, out.dtype) for out in outs),
-            pltpu.SMEM(src_order.shape, jnp.int32),
-            pltpu.SMEM(dst_order.shape, jnp.int32),
-            pltpu.SMEM(doc_lengths.shape, jnp.int32),
+            pltpu.SMEM(order.shape, jnp.int32),
             pltpu.VMEM((n, BR, cols), bf16),
             pltpu.VMEM((n, BR, cols), bf16),
             pltpu.VMEM((rows, cols), bf16),
@@ -570,7 +584,7 @@
             pltpu.VMEM((rows, 2 * HD), f32),
             pltpu.VMEM((nm, kept, 2 * HD), bf16),
             pltpu.VMEM((nm, kept, 2 * HD), bf16),
-            dma((11,)),
+            dma((9,)),
             dma,
             dma,
             dma,
@@ -587,12 +601,10 @@
             dma,
         ],
         compiler_params=pltpu.CompilerParams(
-            collective_id=0, has_side_effects=True, vmem_limit_bytes=60 * 1024 * 1024
+            collective_id=0, has_side_effects=True, vmem_limit_bytes=54784 * 1024
         ),
     )(
-        src_order,
-        dst_order,
-        doc_lengths,
+        order,
         blocks(queries),
         blocks(out_grad),
         attn_out,

time: 120 us -> 115 us (0.958)
  Pallas kernels: 114 us -> 111 us
  local copies, waits for them, and re-layouts: 4.61 us -> 2.65 us
    pallas_call x1, Pallas kernels: 114 us -> 111 us  [body(): pl.pallas_call(functools.partial(kernel, n, nm), out_shape=outs, in_specs...]
    unnamed x3 -> x5, local copies, waits for them, and re-layouts: 4.61 us -> 2.65 us
where the time goes in v3:
time: 115 us
  Pallas kernels  111 us (97%)
  local copies, waits for them, and re-layouts  2.65 us (2%)
    pallas_call x1, Pallas kernels, body(): pl.pallas_call(functools.partial(kernel, n, nm), out_shape=outs, in_specs...  111 us
    unnamed x5, local copies, waits for them, and re-layouts  2.65 us

profile of v3, /device:TPU:1, one launch (start us, length us, event | category | flops | bytes accessed | tf_op | source)
XLA Modules:
  0.0 115.1 jit_solution(18385831023937843733)
XLA Ops:
  0.6 0.8 pad_add_fusion.order_hbm
  1.4 0.0 copy-start
  1.4 0.7 copy-done
  2.1 111.1 %shard_map.130 = (bf16[512,256]{1,0:T(8,128)(2,1)S(1)}, bf16[32,1024]{1,0:T(8,128)(2,1)S(1)}, f32[64,256]{1,0:T(8,128)S(1)}) custom-call(s32[1,136]{1,0:T(1,128)S(1)} %pad_add_fusion.order_hbm, bf16[64,8,256]{2,1,0:T(8,128)(2,1)} %bitcast.10, bf16[64,8,256]{2,1,0:T(8,128)(2,1)} %bitcast.11, bf16[512,256]{1,0:T(8,128)(2,1)} %o_hbm.1, ...), custom_call_target="tpu_custom_call" | custom-call | tf_op jit(solution)/shard_map/pallas_call | solution.py:553
  113.2 0.7 copy.17
  113.9 0.6 copy.18
  114.5 0.6 copy.19
Async XLA Ops:
  1.4 0.7 copy-start
